TPU v7x, 256 devices: a whole 4x4x8 slice. The times are simulated.
256 devices in a mesh: seq: 32 (over y, x, core), head: 8 (over z).
Axes of the slice: x: 4, y: 4, z: 8, core: 2. Of those that a mesh axis runs over, the one named last changes fastest.
Arguments:
- q_values: bfloat16 [65536, 4096], P('seq', 'head'), may hold values from -6 to 6
- k_values: bfloat16 [65536, 4096], P('seq', 'head'), may hold values from -6 to 6
- v_values: bfloat16 [65536, 4096], P('seq', 'head'), may hold values from -6 to 6
- q_scales: float32 [65536, 32], P('seq', 'head'), may hold values from 0.5 to 4
- k_scales: float32 [65536, 32], P('seq', 'head'), may hold values from 0.5 to 4
- v_scales: float32 [65536, 32], P('seq', 'head'), may hold values from 0.5 to 2
- conv_weight: float32 [32, 33], P('head'), may hold values from -0.9 to 0.9
Outputs:
- attended: bfloat16 [65536, 4096], P('seq', 'head')
All inputs are finite; a program needn't handle non-finite values.
Results may differ from a plain program's by a relative error of at most 0.03.
Values may be sent and summed in bfloat16 or wider, within the bound.
A program may use at most 128 MiB of HBM per device.

v0:
```python
import functools
import jax
import jax.numpy as jnp
from jax import lax
from jax.sharding import Mesh
from jax.sharding import PartitionSpec as P

HEAD_DIM = 128
LANDMARKS = 256
SWEEPS = 6
SEQ = ("seq_0", "seq_1", "seq_2")


def side_by_side(arrays, axis, dim, along):
    both = jnp.concatenate(arrays, axis=along)
    result, at, finished = (lax.all_gather(both, axis, axis=dim, tiled=True), 0, [])
    for a in arrays:
        finished.append(lax.slice_in_dim(result, at, at + a.shape[along], axis=along))
        at += a.shape[along]
    return tuple(finished)


def from_everyone(shard, axis):
    copies = jnp.broadcast_to(shard, (lax.axis_size(axis), *shard.shape))
    return lax.all_to_all(copies, axis, split_axis=0, concat_axis=0, tiled=True)


def taken_together(shard, axis):
    everything = from_everyone(shard, axis)
    return jnp.max(everything, axis=0)


def packed_total(arrays, axis):
    line, at, finished = (jnp.concatenate([a.reshape(-1) for a in arrays]), 0, [])
    total = taken_together(line, axis)
    for a in arrays:
        finished.append(total[at : at + a.size].reshape(a.shape))
        at += a.size
    return tuple(finished)


def by_axis(shard, axes):
    return functools.reduce(lax.pmax, axes, shard)


def padded_2(shard, sides, width):
    for axis, dim in sides:
        count, length = (lax.axis_size(axis), shard.shape[dim])
        up = [(i, (i + 1) % count) for i in range(count - 1)]
        down = [(j, i) for i, j in up]
        last = lax.slice_in_dim(shard, length - width, length, axis=dim)
        leading = lax.slice_in_dim(shard, 0, width, axis=dim)
        before = lax.ppermute(last, axis, up)
        after = lax.ppermute(leading, axis, down)
        shard = jnp.concatenate([before, shard, after], axis=dim)
    return shard


def dequant(value_rows, scales):
    count = scales.shape[1]
    shaped = value_rows.reshape(value_rows.shape[0], count, HEAD_DIM).astype(jnp.float32)
    return (shaped * scales[:, :, None]).astype(jnp.bfloat16)


def newton(kernel, initial, right_side):
    eye_matrix = jnp.eye(kernel.shape[0], dtype=jnp.float32)
    iterate = initial
    for sweep in range(SWEEPS):
        product = jnp.dot(kernel, iterate)
        inner_term = 7.0 * eye_matrix - product
        inner_term = 15.0 * eye_matrix - jnp.dot(product, inner_term)
        inner_term = 13.0 * eye_matrix - jnp.dot(product, inner_term)
        iterate = 0.25 * jnp.dot(iterate, inner_term)
    return jnp.dot(iterate, right_side).astype(jnp.bfloat16)


def shards(q_values, k_values, v_values, q_scales, k_scales, v_scales, conv_weight):
    tok_rows = q_values.shape[0]
    head_count = q_scales.shape[1]
    seq_count = lax.axis_size(SEQ)
    marks_here = LANDMARKS // seq_count
    segment = tok_rows // marks_here
    query_rows = dequant(q_values, q_scales)
    key_rows = dequant(k_values, k_scales)
    value_rows = dequant(v_values, v_scales)

    def means(source):
        shaped = source.reshape(marks_here, segment, head_count, HEAD_DIM).astype(jnp.float32)
        return (
            jnp.mean(shaped, axis=1).astype(jnp.bfloat16).reshape(marks_here, head_count * HEAD_DIM)
        )

    query_landmarks, key_landmarks = side_by_side((means(query_rows), means(key_rows)), SEQ, 0, 1)
    query_landmarks = query_landmarks.reshape(LANDMARKS, head_count, HEAD_DIM)
    key_landmarks = key_landmarks.reshape(LANDMARKS, head_count, HEAD_DIM)
    pseudo_inverse_factor = HEAD_DIM ** (-0.5)
    landmark_kernel = (
        jnp.einsum(
            "jvc,kvc->vjk", query_landmarks, key_landmarks, preferred_element_type=jnp.float32
        )
        * pseudo_inverse_factor
    )
    middle = jax.nn.softmax(landmark_kernel, axis=-1)
    col_top = jnp.max(jnp.sum(middle, axis=1))
    row_top = jnp.max(jnp.sum(middle, axis=2))
    col_top, row_top = packed_total((col_top, row_top), "head")
    start = jnp.swapaxes(middle, 1, 2) / (col_top * row_top)
    distant_term = (
        jnp.einsum("kli,nli->lkn", query_landmarks, key_rows, preferred_element_type=jnp.float32)
        * pseudo_inverse_factor
    )
    far_top = by_axis(jnp.max(distant_term, axis=-1), SEQ)
    weight_matrix = jnp.exp(distant_term - far_top[:, :, None])
    total = jnp.sum(weight_matrix, axis=-1)
    summed = jnp.einsum(
        "lnx,xlj->nlj",
        weight_matrix.astype(jnp.bfloat16),
        value_rows,
        preferred_element_type=jnp.float32,
    )
    total, summed = (
        lax.psum(total.astype(jnp.bfloat16), SEQ).astype(jnp.float32),
        lax.psum(summed.astype(jnp.bfloat16), SEQ).astype(jnp.float32),
    )
    reduced = summed / jnp.swapaxes(total, 0, 1)[:, :, None]
    projected_values = jax.vmap(newton, in_axes=(0, 0, 1), out_axes=1)(middle, start, reduced)
    near_scores = (
        jnp.einsum("zea,uea->ezu", query_rows, key_landmarks, preferred_element_type=jnp.float32)
        * pseudo_inverse_factor
    )
    local_term = jax.nn.softmax(near_scores, axis=-1).astype(jnp.bfloat16)
    attended = jnp.einsum(
        "kbv,vkg->bkg", local_term, projected_values, preferred_element_type=jnp.float32
    ).reshape(tok_rows, head_count * HEAD_DIM)
    flat_values = value_rows.reshape(tok_rows, head_count * HEAD_DIM)
    tap_count = conv_weight.shape[1]
    padded = padded_2(flat_values, ((SEQ, 0),), tap_count // 2)
    tap_table = jnp.repeat(conv_weight, HEAD_DIM, axis=0)
    mixed = jnp.zeros((tok_rows, head_count * HEAD_DIM), jnp.float32)
    for tap_index in range(tap_count):
        mixed = (
            mixed
            + padded[tap_index : tap_index + tok_rows].astype(jnp.float32) * tap_table[:, tap_index]
        )
    return (attended + mixed).astype(jnp.bfloat16)


def solution(mesh):
    finer = Mesh(
        mesh.devices.reshape(4, 4, 2, mesh.shape["head"]), ("seq_0", "seq_1", "seq_2", "head")
    )
    placed = (
        P(SEQ, "head"),
        P(SEQ, "head"),
        P(SEQ, "head"),
        P(SEQ, "head"),
        P(SEQ, "head"),
        P(SEQ, "head"),
        P("head", None),
    )
    return jax.shard_map(
        shards, mesh=finer, in_specs=placed, out_specs=P(SEQ, "head"), check_vma=False
    )
```

profile of v0, /device:TPU:32, one launch (start us, length us, event | category | flops | bytes accessed | tf_op | source)
XLA Modules:
  0.0 302.6 jit_solution(4559212239840184039)
XLA Ops:
  6.5 4.7 %reshape.126 = f32[8,256,4,128]{3,2,1,0:T(4,128)} reshape(bf16[2048,512]{1,0:T(8,128)(2,1)} %param.7) | data formatting | bytes 6291456 | tf_op jit(solution)/shard_map/convert_element_type | solution.py:61
  11.3 0.4 copy.104
  11.7 4.6 %convert_reduce_fusion.1 = f32[8,4,128]{2,1,0:T(4,128)S(1)} fusion(f32[8,256,4,128]{3,2,1,0:T(4,128)} %reshape.126, f32[8,256,4]{2,1,0:T(8,128)S(1)} %bitcast.119), kind=kLoop, calls=%fused_computation.52 | loop fusion | flops 4190208 | bytes 4243456 | tf_op jit(solution)/shard_map/reduce_sum | solution.py:90
  16.3 3.0 reshape.127
  19.3 0.4 copy.105
  19.6 4.4 %convert_reduce_fusion = f32[8,4,128]{2,1,0:T(4,128)S(1)} fusion(f32[8,256,4,128]{3,2,1,0:T(4,128)} %reshape.127, f32[8,256,4]{2,1,0:T(8,128)S(1)} %bitcast.120), kind=kLoop, calls=%fused_computation.50 | loop fusion | flops 4190208 | bytes 4243456 | tf_op jit(solution)/shard_map/reduce_sum | solution.py:90
  24.1 25.1 %all_gather.3 = bf16[256,1024]{1,0:T(8,128)(2,1)S(1)} all-gather(bf16[8,1024]{1,0:T(8,128)(2,1)S(1)} %pad_maximum_fusion.2), channel_id=1, replica_groups=mesh['seq_0'=4,'seq_1'=4,'seq_2'=2,'head'=8] {'seq_0','seq_1','seq_2'}, dimensions={0}, use_global_device_ids=true | all-gather | bytes 540672 | tf_op jit(solution)/shard_map/all_gather | solution.py:16
  49.2 0.1 copy.111
  49.3 0.8 copy.112
  50.2 1.4 fusion.169
  51.6 0.4 fusion.127
  52.0 0.5 fusion.163
  52.5 0.7 reduce_max.55
  53.2 0.6 reduce_max.56
  53.8 1.3 pad_maximum_fusion.3
  55.1 0.6 broadcast_in_dim.4
  55.7 8.6 %all-to-all-start = ((f32[8,1,2]{2,1,0:T(1,128)}), f32[8,1,2]{2,1,0:T(1,128)S(1)}, u32[]{:S(2)}, u32[]{:S(2)}) async-start(f32[8,1,2]{2,1,0:T(1,128)} %broadcast_in_dim.4), calls=%async_computation | async-start | bytes 8192 | tf_op jit(solution)/shard_map/all_to_all | solution.py:25
  64.3 4.4 %multiply_reduce_fusion = (f32[4,256]{1,0:T(4,128)S(1)}, f32[4,256,2048]{2,1,0:T(8,128)}) fusion(bf16[256,4,128]{0,2,1:T(8,128)(2,1)S(1)} %bitcast.123, f32[2048,4]{0,1:T(4,128)S(1)} %copy-done.11, bf16[2048,512]{1,0:T(8,128)(2,1)S(1)} %copy-done.4), kind=kOutput, calls=%fused_computation.34 | convolution fusion | flops 544209920 | bytes 10784768 | tf_op jit(solution)/shard_map/kli,nli->lkn/dot_general | solution.py:109
  68.7 10.2 %pmax.21 = f32[4,256]{1,0:T(4,128)S(1)} all-reduce(f32[4,256]{1,0:T(4,128)S(1)} %get-tuple-element.48), channel_id=1, replica_groups=mesh['seq_0'=4,'seq_1'=4,'seq_2'=2,'head'=8] {'seq_0'}, use_global_device_ids=true, to_apply=%region_10.0 | all-reduce | flops 1024 | bytes 8192 | tf_op jit(solution)/shard_map/pmax | solution.py:43
  78.9 8.5 %pmax.22 = f32[4,256]{1,0:T(4,128)S(1)} all-reduce(f32[4,256]{1,0:T(4,128)S(1)} %pmax.21), channel_id=1, replica_groups=mesh['seq_0'=4,'seq_1'=4,'seq_2'=2,'head'=8] {'seq_1'}, use_global_device_ids=true, to_apply=%region_11.0 | all-reduce | flops 1024 | bytes 8192 | tf_op jit(solution)/shard_map/pmax | solution.py:43
  87.5 2.5 pmax.23
  90.0 4.1 %copy.106 = f32[2048,512]{0,1:T(8,128)} copy(bf16[2048,512]{1,0:T(8,128)(2,1)} %param.9) | data formatting | bytes 6291456 | tf_op jit(solution)/shard_map/convert_element_type | solution.py:61
  94.1 2.7 multiply_convert_fusion.1
  96.8 5.9 %fusion.121 = bf16[256,4,128]{0,2,1:T(8,128)(2,1)} fusion(bf16[2048,4,128]{0,2,1:T(8,128)(2,1)S(1)} %multiply_convert_fusion.1, f32[4,256,2048]{2,1,0:T(8,128)} %get-tuple-element.49, f32[4,256]{1,0:T(4,128)S(1)} %pmax.23), kind=kOutput, calls=%fused_computation.148 | convolution fusion | flops 543293440 | bytes 10752000 | tf_op jit(solution)/shard_map/lnx,xlj->nlj/dot_general | solution.py:115
  102.7 0.0 all-reduce.2.cloned.1.call-update
  102.7 0.1 fusion.164
  102.8 0.1 copy.107
  102.9 2.1 collective-permute-start
  105.0 0.1 copy.109
  105.1 1.5 collective-permute-start.1
  106.6 4.4 %fusion.2 = bf16[4,256]{1,0:T(4,128)(2,1)S(1)} fusion(f32[4,256,2048]{2,1,0:T(8,128)} %get-tuple-element.49, f32[4,256]{1,0:T(4,128)S(1)} %pmax.23), kind=kLoop, calls=%fused_computation.37 | loop fusion | flops 6290432 | bytes 8394752 | tf_op jit(solution)/shard_map/reduce_sum | solution.py:114
  111.1 4.2 %fusion.16 = f32[4,2048,256]{1,2,0:T(8,128)} fusion(bf16[256,4,128]{0,2,1:T(8,128)(2,1)S(1)} %bitcast.125, f32[2048,4]{0,1:T(4,128)S(1)} %copy-done.12, bf16[2048,512]{1,0:T(8,128)(2,1)S(1)} %copy-done.5), kind=kOutput, calls=%fused_computation.56 | convolution fusion | flops 540016640 | bytes 10780672 | tf_op jit(solution)/shard_map/zea,uea->ezu/dot_general | solution.py:128
  115.3 0.1 copy.92
  115.4 0.1 broadcast_bitcast_fusion
  115.6 0.7 fusion.166
  116.3 0.6 fusion.167
  116.9 11.7 %fusion.170 = (f32[4,2048]{1,0:T(4,128)S(1)}, f32[4,2048,256]{1,2,0:T(8,128)}) fusion(f32[4,2048,256]{1,2,0:T(8,128)} %fusion.16), kind=kOutput, calls=%fused_computation.199 | output fusion | flops 8388863 | bytes 16809984 | tf_op jit(solution)/shard_map/sub | solution.py:131
  128.6 2.5 mul.490
  131.1 5.3 %copy.108 = f32[2048,512]{1,0:T(8,128)} copy(f32[2048,512]{0,1:T(8,128)} %bitcast.118) | data formatting | bytes 8388608 | tf_op jit(solution)/shard_map/mul | solution.py:62
  136.5 4.9 %multiply_convert_fusion = bf16[2048,512]{1,0:T(8,128)(2,1)} fusion(f32[2048,512]{1,0:T(8,128)} %copy.108, bf16[2048,512]{1,0:T(8,128)(2,1)} %param.9), kind=kLoop, calls=%fused_computation.45 | loop fusion | flops 3145728 | bytes 8388608 | tf_op jit(solution)/shard_map/convert_element_type | solution.py:62
  141.4 64.7 %psum.15 = bf16[256,4]{0,1:T(4,128)(2,1)S(1)} all-reduce(bf16[256,4]{0,1:T(4,128)(2,1)S(1)} %bitcast.164), channel_id=1, replica_groups=mesh['seq_0'=4,'seq_1'=4,'seq_2'=2,'head'=8] {'seq_0','seq_1','seq_2'}, use_global_device_ids=true, to_apply=%region_15.0 | all-reduce | flops 1024 | bytes 4096 | tf_op jit(solution)/shard_map/psum | solution.py:122
  206.1 0.7 fusion.168
  208.1 1.4 fusion.150
  209.5 0.5 fusion.68
  210.0 1.8 convolution_multiply_fusion.5
  211.8 4.3 %online-softmax = f32[4,256,256]{2,1,0:T(8,128)} custom-call(f32[4,256,256]{2,1,0:T(8,128)} %copy-done, f32[4,256,256]{2,1,0:T(8,128)} %convolution_multiply_fusion.5), custom_call_target="tpu_custom_call" | custom-call | tf_op online-softmax
  216.2 2.6 fusion.77
  218.8 1.4 convolution_multiply_fusion.4
  220.2 4.3 %online-softmax.1 = f32[4,256,256]{2,1,0:T(8,128)} custom-call(f32[4,256,256]{2,1,0:T(8,128)} %copy-done, f32[4,256,256]{2,1,0:T(8,128)} %convolution_multiply_fusion.4), custom_call_target="tpu_custom_call" | custom-call | tf_op online-softmax
  224.5 2.6 fusion.86
  227.1 1.4 convolution_multiply_fusion.3
  228.5 4.3 %online-softmax.2 = f32[4,256,256]{2,1,0:T(8,128)} custom-call(f32[4,256,256]{2,1,0:T(8,128)} %copy-done, f32[4,256,256]{2,1,0:T(8,128)} %convolution_multiply_fusion.3), custom_call_target="tpu_custom_call" | custom-call | tf_op online-softmax
  232.8 2.6 fusion.95
  235.4 1.4 convolution_multiply_fusion.2
  236.8 4.3 %online-softmax.3 = f32[4,256,256]{2,1,0:T(8,128)} custom-call(f32[4,256,256]{2,1,0:T(8,128)} %copy-done, f32[4,256,256]{2,1,0:T(8,128)} %convolution_multiply_fusion.2), custom_call_target="tpu_custom_call" | custom-call | tf_op online-softmax
  241.1 2.6 fusion.104
  243.7 1.4 convolution_multiply_fusion.1
  245.1 4.3 %online-softmax.4 = f32[4,256,256]{2,1,0:T(8,128)} custom-call(f32[4,256,256]{2,1,0:T(8,128)} %copy-done, f32[4,256,256]{2,1,0:T(8,128)} %convolution_multiply_fusion.1), custom_call_target="tpu_custom_call" | custom-call | tf_op online-softmax
  249.5 2.6 fusion.113
  252.1 0.0 all-reduce.2.cloned.1.call-done
  252.1 1.4 fusion.124
  253.5 6.3 %fusion.13 = f32[4,128,2048]{2,1,0:T(8,128)} fusion(bf16[256,4,128]{2,0,1:T(8,128)(2,1)S(1)} %fusion.124, f32[4,2048,256]{1,2,0:T(8,128)} %get-tuple-element.51, f32[4,2048]{1,0:T(4,128)S(1)} %get-tuple-element.50), kind=kOutput, calls=%fused_computation.54 | convolution fusion | flops 541065216 | bytes 12877824 | tf_op jit(solution)/shard_map/kbv,vkg->bkg/dot_general | solution.py:132
  260.0 5.5 %copy.94 = f32[2048,512]{1,0:T(8,128)} copy(f32[2048,512]{0,1:T(8,128)} %bitcast.121) | data formatting | bytes 8388608 | tf_op jit(solution)/shard_map/reshape | solution.py:134
  265.9 29.8 %add_convert_fusion = bf16[2048,512]{1,0:T(8,128)(2,1)} fusion(f32[2048,512]{1,0:T(8,128)} %copy.94, bf16[2048,512]{1,0:T(8,128)(2,1)S(1)} %copy-done.6, bf16[16,512]{1,0:T(8,128)(2,1)S(1)} %collective-permute-done.1, bf16[16,512]{1,0:T(8,128)(2,1)S(1)} %collective-permute-done, f32[512]{0:T(512)S(1)} %bitcast.132, f32[512]{0:T(512)S(1)} %bitcast.133, ...), kind=kLoop, calls=%fused_computation.44 | loop fusion | flops 205520896 | bytes 8488960 | tf_op jit(solution)/shard_map/convert_element_type | solution.py:145
  (108 shorter events, 0.4 us)
Async XLA Ops:
  6.5 4.7 %copy-start.12 = (f32[2048,4]{0,1:T(4,128)S(1)}, f32[2048,4]{0,1:T(4,128)}, u32[]{:S(2)}) copy-start(f32[2048,4]{0,1:T(4,128)} %param.10) | copy-start | bytes 98308
  11.3 5.0 %copy-start.4 = (bf16[2048,512]{1,0:T(8,128)(2,1)S(1)}, bf16[2048,512]{1,0:T(8,128)(2,1)}, u32[]{:S(2)}) copy-start(bf16[2048,512]{1,0:T(8,128)(2,1)} %param.8) | copy-start | bytes 6291460
  16.2 3.1 %copy-start.11 = (f32[2048,4]{0,1:T(4,128)S(1)}, f32[2048,4]{0,1:T(4,128)}, u32[]{:S(2)}) copy-start(f32[2048,4]{0,1:T(4,128)} %param.11) | copy-start | bytes 98308
  51.6 158.4 %copy-start = (f32[4,256,256]{2,1,0:T(8,128)}, f32[4,256,256]{2,1,0:T(8,128)S(1)}, u32[]{:S(2)}) copy-start(f32[4,256,256]{2,1,0:T(8,128)S(1)} %get-tuple-element.47) | copy-start | bytes 3145732
  55.7 150.4 %all-to-all-start = ((f32[8,1,2]{2,1,0:T(1,128)}), f32[8,1,2]{2,1,0:T(1,128)S(1)}, u32[]{:S(2)}, u32[]{:S(2)}) async-start(f32[8,1,2]{2,1,0:T(1,128)} %broadcast_in_dim.4), calls=%async_computation | async-start | bytes 8192 | tf_op jit(solution)/shard_map/all_to_all | solution.py:25
  64.3 187.8 %all-reduce.2.cloned.1.call-start = ((), (), s32[]{:S(2)}) async-start(), calls=%async_computation.1 | async-start | bytes 524288 | tf_op jit(solution)/shard_map/psum | solution.py:123
  68.7 25.4 %copy-start.10 = (f32[2048,4]{0,1:T(4,128)S(1)}, f32[2048,4]{0,1:T(4,128)}, u32[]{:S(2)}) copy-start(f32[2048,4]{0,1:T(4,128)} %param.12) | copy-start | bytes 98308
  102.9 162.7 %collective-permute-start = (bf16[16,512]{1,0:T(8,128)(2,1)S(1)}, bf16[16,512]{1,0:T(8,128)(2,1)S(1)}, u32[]{:S(2)}, u32[]{:S(2)}) collective-permute-start(bf16[16,512]{1,0:T(8,128)(2,1)S(1)} %copy.107), channel_id=1, source_target_pairs={{0,8},{8,16},{16,24},{24,32},{32,40},{40,48},{48,56},{56,64},{64,7... | collective-permute-start | bytes 49160 | tf_op jit(solution)/shard_map/ppermute | solution.py:53
  105.1 160.5 %collective-permute-start.1 = (bf16[16,512]{1,0:T(8,128)(2,1)S(1)}, bf16[16,512]{1,0:T(8,128)(2,1)S(1)}, u32[]{:S(2)}, u32[]{:S(2)}) collective-permute-start(bf16[16,512]{1,0:T(8,128)(2,1)S(1)} %copy.109), channel_id=1, source_target_pairs={{8,0},{16,8},{24,16},{32,24},{40,32},{48,40},{56,48},{64,56},{72,6... | collective-permute-start | bytes 49160 | tf_op jit(solution)/shard_map/ppermute | solution.py:54
  106.6 4.5 %copy-start.5 = (bf16[2048,512]{1,0:T(8,128)(2,1)S(1)}, bf16[2048,512]{1,0:T(8,128)(2,1)}, u32[]{:S(2)}) copy-start(bf16[2048,512]{1,0:T(8,128)(2,1)} %param.7) | copy-start | bytes 6291460
  106.6 4.5 %copy-start.9 = (bf16[256,512]{0,1:T(8,128)(2,1)S(1)}, bf16[256,512]{0,1:T(8,128)(2,1)}, u32[]{:S(2)}) copy-start(bf16[256,512]{0,1:T(8,128)(2,1)} %copy.112) | copy-start | bytes 786436
  111.1 4.3 %copy-start.45 = (f32[4,33]{1,0:T(4,128)S(1)}, f32[4,33]{1,0:T(4,128)}, u32[]{:S(2)}) copy-start(f32[4,33]{1,0:T(4,128)} %param.13) | copy-start | bytes 1588
  211.8 6.9 %copy-start.8 = (f32[4,256,256]{2,1,0:T(8,128)S(1)}, f32[4,256,256]{2,1,0:T(8,128)}, u32[]{:S(2)}) copy-start(f32[4,256,256]{2,1,0:T(8,128)} %convolution_multiply_fusion.5) | copy-start | bytes 3145732
  220.2 6.9 %copy-start.1 = (f32[4,256,256]{2,1,0:T(8,128)S(1)}, f32[4,256,256]{2,1,0:T(8,128)}, u32[]{:S(2)}) copy-start(f32[4,256,256]{2,1,0:T(8,128)} %convolution_multiply_fusion.4) | copy-start | bytes 3145732
  228.5 6.9 %copy-start.2 = (f32[4,256,256]{2,1,0:T(8,128)S(1)}, f32[4,256,256]{2,1,0:T(8,128)}, u32[]{:S(2)}) copy-start(f32[4,256,256]{2,1,0:T(8,128)} %convolution_multiply_fusion.3) | copy-start | bytes 3145732
  236.8 6.9 %copy-start.3 = (f32[4,256,256]{2,1,0:T(8,128)S(1)}, f32[4,256,256]{2,1,0:T(8,128)}, u32[]{:S(2)}) copy-start(f32[4,256,256]{2,1,0:T(8,128)} %convolution_multiply_fusion.2) | copy-start | bytes 3145732
  245.1 7.0 %copy-start.7 = (f32[4,256,256]{2,1,0:T(8,128)S(1)}, f32[4,256,256]{2,1,0:T(8,128)}, u32[]{:S(2)}) copy-start(f32[4,256,256]{2,1,0:T(8,128)} %convolution_multiply_fusion.1) | copy-start | bytes 3145732
  259.7 5.8 %copy-start.6 = (bf16[2048,512]{1,0:T(8,128)(2,1)S(1)}, bf16[2048,512]{1,0:T(8,128)(2,1)}, u32[]{:S(2)}) copy-start(bf16[2048,512]{1,0:T(8,128)(2,1)} %multiply_convert_fusion) | copy-start | bytes 6291460
  259.7 5.8 %copy-start.13 = (f32[512,1]{0,1:T(1,128)S(1)}, f32[512,1]{0,1:T(1,128)}, u32[]{:S(2)}) copy-start(f32[512,1]{0,1:T(1,128)} %get-tuple-element.12) | copy-start | bytes 6148
  259.7 5.8 %copy-start.14 = (f32[512,1]{0,1:T(1,128)S(1)}, f32[512,1]{0,1:T(1,128)}, u32[]{:S(2)}) copy-start(f32[512,1]{0,1:T(1,128)} %get-tuple-element.13) | copy-start | bytes 6148
  259.7 5.8 %copy-start.15 = (f32[512,1]{0,1:T(1,128)S(1)}, f32[512,1]{0,1:T(1,128)}, u32[]{:S(2)}) copy-start(f32[512,1]{0,1:T(1,128)} %get-tuple-element.14) | copy-start | bytes 6148
  259.8 5.9 %copy-start.16 = (f32[512,1]{0,1:T(1,128)S(1)}, f32[512,1]{0,1:T(1,128)}, u32[]{:S(2)}) copy-start(f32[512,1]{0,1:T(1,128)} %get-tuple-element.15) | copy-start | bytes 6148
  259.8 5.9 %copy-start.17 = (f32[512,1]{0,1:T(1,128)S(1)}, f32[512,1]{0,1:T(1,128)}, u32[]{:S(2)}) copy-start(f32[512,1]{0,1:T(1,128)} %get-tuple-element.16) | copy-start | bytes 6148
  259.8 5.9 %copy-start.18 = (f32[512,1]{0,1:T(1,128)S(1)}, f32[512,1]{0,1:T(1,128)}, u32[]{:S(2)}) copy-start(f32[512,1]{0,1:T(1,128)} %get-tuple-element.17) | copy-start | bytes 6148
  259.8 5.9 %copy-start.19 = (f32[512,1]{0,1:T(1,128)S(1)}, f32[512,1]{0,1:T(1,128)}, u32[]{:S(2)}) copy-start(f32[512,1]{0,1:T(1,128)} %get-tuple-element.18) | copy-start | bytes 6148
  259.8 5.9 %copy-start.20 = (f32[512,1]{0,1:T(1,128)S(1)}, f32[512,1]{0,1:T(1,128)}, u32[]{:S(2)}) copy-start(f32[512,1]{0,1:T(1,128)} %get-tuple-element.19) | copy-start | bytes 6148
  259.8 5.9 %copy-start.21 = (f32[512,1]{0,1:T(1,128)S(1)}, f32[512,1]{0,1:T(1,128)}, u32[]{:S(2)}) copy-start(f32[512,1]{0,1:T(1,128)} %get-tuple-element.20) | copy-start | bytes 6148
  259.8 5.9 %copy-start.22 = (f32[512,1]{0,1:T(1,128)S(1)}, f32[512,1]{0,1:T(1,128)}, u32[]{:S(2)}) copy-start(f32[512,1]{0,1:T(1,128)} %get-tuple-element.21) | copy-start | bytes 6148
  259.8 5.9 %copy-start.23 = (f32[512,1]{0,1:T(1,128)S(1)}, f32[512,1]{0,1:T(1,128)}, u32[]{:S(2)}) copy-start(f32[512,1]{0,1:T(1,128)} %get-tuple-element.22) | copy-start | bytes 6148
  259.8 5.9 %copy-start.24 = (f32[512,1]{0,1:T(1,128)S(1)}, f32[512,1]{0,1:T(1,128)}, u32[]{:S(2)}) copy-start(f32[512,1]{0,1:T(1,128)} %get-tuple-element.23) | copy-start | bytes 6148
  259.8 5.9 %copy-start.25 = (f32[512,1]{0,1:T(1,128)S(1)}, f32[512,1]{0,1:T(1,128)}, u32[]{:S(2)}) copy-start(f32[512,1]{0,1:T(1,128)} %get-tuple-element.24) | copy-start | bytes 6148
  259.9 5.9 %copy-start.26 = (f32[512,1]{0,1:T(1,128)S(1)}, f32[512,1]{0,1:T(1,128)}, u32[]{:S(2)}) copy-start(f32[512,1]{0,1:T(1,128)} %get-tuple-element.25) | copy-start | bytes 6148
  259.9 5.9 %copy-start.27 = (f32[512,1]{0,1:T(1,128)S(1)}, f32[512,1]{0,1:T(1,128)}, u32[]{:S(2)}) copy-start(f32[512,1]{0,1:T(1,128)} %get-tuple-element.26) | copy-start | bytes 6148
  259.9 5.9 %copy-start.28 = (f32[512,1]{0,1:T(1,128)S(1)}, f32[512,1]{0,1:T(1,128)}, u32[]{:S(2)}) copy-start(f32[512,1]{0,1:T(1,128)} %get-tuple-element.27) | copy-start | bytes 6148
  259.9 5.9 %copy-start.29 = (f32[512,1]{0,1:T(1,128)S(1)}, f32[512,1]{0,1:T(1,128)}, u32[]{:S(2)}) copy-start(f32[512,1]{0,1:T(1,128)} %get-tuple-element.28) | copy-start | bytes 6148
  259.9 5.9 %copy-start.30 = (f32[512,1]{0,1:T(1,128)S(1)}, f32[512,1]{0,1:T(1,128)}, u32[]{:S(2)}) copy-start(f32[512,1]{0,1:T(1,128)} %get-tuple-element.29) | copy-start | bytes 6148
  259.9 5.9 %copy-start.31 = (f32[512,1]{0,1:T(1,128)S(1)}, f32[512,1]{0,1:T(1,128)}, u32[]{:S(2)}) copy-start(f32[512,1]{0,1:T(1,128)} %get-tuple-element.30) | copy-start | bytes 6148
  259.9 5.9 %copy-start.32 = (f32[512,1]{0,1:T(1,128)S(1)}, f32[512,1]{0,1:T(1,128)}, u32[]{:S(2)}) copy-start(f32[512,1]{0,1:T(1,128)} %get-tuple-element.31) | copy-start | bytes 6148
  259.9 5.9 %copy-start.33 = (f32[512,1]{0,1:T(1,128)S(1)}, f32[512,1]{0,1:T(1,128)}, u32[]{:S(2)}) copy-start(f32[512,1]{0,1:T(1,128)} %get-tuple-element.32) | copy-start | bytes 6148
  259.9 5.9 %copy-start.34 = (f32[512,1]{0,1:T(1,128)S(1)}, f32[512,1]{0,1:T(1,128)}, u32[]{:S(2)}) copy-start(f32[512,1]{0,1:T(1,128)} %get-tuple-element.33) | copy-start | bytes 6148
  259.9 5.9 %copy-start.35 = (f32[512,1]{0,1:T(1,128)S(1)}, f32[512,1]{0,1:T(1,128)}, u32[]{:S(2)}) copy-start(f32[512,1]{0,1:T(1,128)} %get-tuple-element.34) | copy-start | bytes 6148
  259.9 5.9 %copy-start.36 = (f32[512,1]{0,1:T(1,128)S(1)}, f32[512,1]{0,1:T(1,128)}, u32[]{:S(2)}) copy-start(f32[512,1]{0,1:T(1,128)} %get-tuple-element.35) | copy-start | bytes 6148
  260.0 5.9 %copy-start.37 = (f32[512,1]{0,1:T(1,128)S(1)}, f32[512,1]{0,1:T(1,128)}, u32[]{:S(2)}) copy-start(f32[512,1]{0,1:T(1,128)} %get-tuple-element.36) | copy-start | bytes 6148
  260.0 5.9 %copy-start.38 = (f32[512,1]{0,1:T(1,128)S(1)}, f32[512,1]{0,1:T(1,128)}, u32[]{:S(2)}) copy-start(f32[512,1]{0,1:T(1,128)} %get-tuple-element.37) | copy-start | bytes 6148
  260.0 5.9 %copy-start.39 = (f32[512,1]{0,1:T(1,128)S(1)}, f32[512,1]{0,1:T(1,128)}, u32[]{:S(2)}) copy-start(f32[512,1]{0,1:T(1,128)} %get-tuple-element.38) | copy-start | bytes 6148
  260.0 5.9 %copy-start.40 = (f32[512,1]{0,1:T(1,128)S(1)}, f32[512,1]{0,1:T(1,128)}, u32[]{:S(2)}) copy-start(f32[512,1]{0,1:T(1,128)} %get-tuple-element.39) | copy-start | bytes 6148
  260.0 5.9 %copy-start.41 = (f32[512,1]{0,1:T(1,128)S(1)}, f32[512,1]{0,1:T(1,128)}, u32[]{:S(2)}) copy-start(f32[512,1]{0,1:T(1,128)} %get-tuple-element.40) | copy-start | bytes 6148
  260.0 5.9 %copy-start.42 = (f32[512,1]{0,1:T(1,128)S(1)}, f32[512,1]{0,1:T(1,128)}, u32[]{:S(2)}) copy-start(f32[512,1]{0,1:T(1,128)} %get-tuple-element.41) | copy-start | bytes 6148
  260.0 5.9 %copy-start.43 = (f32[512,1]{0,1:T(1,128)S(1)}, f32[512,1]{0,1:T(1,128)}, u32[]{:S(2)}) copy-start(f32[512,1]{0,1:T(1,128)} %get-tuple-element.42) | copy-start | bytes 6148
  260.0 5.9 %copy-start.44 = (f32[512,1]{0,1:T(1,128)S(1)}, f32[512,1]{0,1:T(1,128)}, u32[]{:S(2)}) copy-start(f32[512,1]{0,1:T(1,128)} %get-tuple-element.43) | copy-start | bytes 6148
Sparse Core Ops, SparseCore 0:
  102.8 108.5 all-reduce.1
where the time goes:
time: 304 us; the launch traced here: 303 us
  blocking collectives  111 us (37%)
  other arithmetic  66.2 us (22%)
  matrix products  45.7 us (15%)
  local copies, waits for them, and re-layouts  30.2 us (10%)
  Pallas kernels  21.7 us (7%)
  between operations  15.5 us (5%)
  starting transfers between devices  12.1 us (4%)
    psum x1, blocking collectives, shards(): lax.psum(total.astype(jnp.bfloat16), SEQ).astype(jnp.float32)  64.7 us
    convert_element_type x1, other arithmetic, shards(): return (attended + mixed).astype(jnp.bfloat16)  29.8 us
    all_gather x1, blocking collectives, side_by_side(): lax.all_gather(both, axis, axis=dim, tiled=True)  25.1 us
    unnamed x5, Pallas kernels  21.7 us
    pmax x3, blocking collectives, by_axis(): return functools.reduce(lax.pmax, axes, shard)  21.3 us
    dot_general x6, matrix products, newton(): inner_term = 13.0 * eye_matrix - jnp.dot(product, inner_term)  13.4 us
    convert_element_type x3, local copies, waits for them, and re-layouts, dequant(): value_rows.reshape(value_rows.shape[0], count, HEAD_DIM).astype(jnp.float32)  11.9 us
    sub x1, other arithmetic, shards(): local_term = jax.nn.softmax(near_scores, axis=-1).astype(jnp.bfloat16)  11.7 us
  transfers between devices with their start and end apart: 4, of which 0 were waited for; matrix products, arithmetic and copies ran while one was open for 29% of the time, Pallas kernels for 7%

commit v1 on v0

--- a/solution.py
+++ b/solution.py
@@ -119,7 +119,9 @@
         preferred_element_type=jnp.float32,
     )
     total, summed = (
-        lax.psum(total.astype(jnp.bfloat16), SEQ).astype(jnp.float32),
+        lax.psum(lax.psum(total.astype(jnp.bfloat16), "seq_0"), ("seq_1", "seq_2")).astype(
+            jnp.float32
+        ),
         lax.psum(summed.astype(jnp.bfloat16), SEQ).astype(jnp.float32),
     )
     reduced = summed / jnp.swapaxes(total, 0, 1)[:, :, None]

time: 304 us -> 265 us (0.87)
  blocking collectives: 111 us -> 72.2 us
    psum x1 -> x2, blocking collectives: 64.7 us -> 25.9 us  [the longest x1 13.5 us: shards(): lax.psum(total.astype(jnp.bfloat16), 'seq_0')]
  transfers between devices with their start and end apart: 4 -> 4, of which waited for: 0 -> 0; matrix products, arithmetic and copies ran while one was open for 29% -> 33% of each run, Pallas kernels for 7% -> 8%
where the time goes in v1:
time: 265 us; the launch traced here: 263 us
  blocking collectives  72.2 us (27%)
  other arithmetic  66.1 us (25%)
  matrix products  45.3 us (17%)
  local copies, waits for them, and re-layouts  30.3 us (11%)
  Pallas kernels  21.5 us (8%)
  between operations  15.6 us (6%)
  starting transfers between devices  11.9 us (4%)
    convert_element_type x1, other arithmetic, shards(): return (attended + mixed).astype(jnp.bfloat16)  29.8 us
    all_gather x1, blocking collectives, side_by_side(): lax.all_gather(both, axis, axis=dim, tiled=True)  25.1 us
    unnamed x5, Pallas kernels  21.5 us
    pmax x3, blocking collectives, by_axis(): return functools.reduce(lax.pmax, axes, shard)  21.3 us
    psum x1, blocking collectives, shards(): lax.psum(total.astype(jnp.bfloat16), 'seq_0')  13.5 us
    dot_general x6, matrix products, newton(): inner_term = 13.0 * eye_matrix - jnp.dot(product, inner_term)  13.2 us
    psum x1, blocking collectives, shards(): lax.psum(lax.psum(total.astype(jnp.bfloat16), 'seq_0'), ('seq_1', 'seq_2'))  12.4 us
    convert_element_type x3, local copies, waits for them, and re-layouts, dequant(): value_rows.reshape(value_rows.shape[0], count, HEAD_DIM).astype(jnp.float32)  11.9 us
  transfers between devices with their start and end apart: 4, of which 0 were waited for; matrix products, arithmetic and copies ran while one was open for 33% of the time, Pallas kernels for 8%

profile of v1, /device:TPU:32, one launch (start us, length us, event | category | flops | bytes accessed | tf_op | source)
XLA Modules:
  0.0 263.0 jit_solution(11794737422688161686)
XLA Ops:
  6.5 4.7 %reshape.126 = f32[8,256,4,128]{3,2,1,0:T(4,128)} reshape(bf16[2048,512]{1,0:T(8,128)(2,1)} %param.7) | data formatting | bytes 6291456 | tf_op jit(solution)/shard_map/convert_element_type | solution.py:61
  11.3 0.4 copy.104
  11.6 4.6 %convert_reduce_fusion.1 = f32[8,4,128]{2,1,0:T(4,128)S(1)} fusion(f32[8,256,4,128]{3,2,1,0:T(4,128)} %reshape.126, f32[8,256,4]{2,1,0:T(8,128)S(1)} %bitcast.117), kind=kLoop, calls=%fused_computation.52 | loop fusion | flops 4190208 | bytes 4243456 | tf_op jit(solution)/shard_map/reduce_sum | solution.py:90
  16.2 3.0 %reshape.127 = f32[8,256,4,128]{3,2,1,0:T(4,128)} reshape(bf16[2048,512]{1,0:T(8,128)(2,1)S(1)} %copy-done.4) | data formatting | bytes 6291456 | tf_op jit(solution)/shard_map/convert_element_type | solution.py:61
  19.3 0.4 copy.105
  19.6 4.4 %convert_reduce_fusion = f32[8,4,128]{2,1,0:T(4,128)S(1)} fusion(f32[8,256,4,128]{3,2,1,0:T(4,128)} %reshape.127, f32[8,256,4]{2,1,0:T(8,128)S(1)} %bitcast.118), kind=kLoop, calls=%fused_computation.50 | loop fusion | flops 4190208 | bytes 4243456 | tf_op jit(solution)/shard_map/reduce_sum | solution.py:90
  24.1 25.1 %all_gather.3 = bf16[256,1024]{1,0:T(8,128)(2,1)S(1)} all-gather(bf16[8,1024]{1,0:T(8,128)(2,1)S(1)} %pad_maximum_fusion.2), channel_id=1, replica_groups=mesh['seq_0'=4,'seq_1'=4,'seq_2'=2,'head'=8] {'seq_0','seq_1','seq_2'}, dimensions={0}, use_global_device_ids=true | all-gather | bytes 540672 | tf_op jit(solution)/shard_map/all_gather | solution.py:16
  49.2 0.1 copy.111
  49.3 0.8 copy.112
  50.2 1.4 fusion.169
  51.6 0.4 fusion.127
  52.0 0.5 fusion.163
  52.5 0.7 reduce_max.55
  53.2 0.6 reduce_max.56
  53.8 1.3 pad_maximum_fusion.3
  55.1 0.6 broadcast_in_dim.4
  55.7 8.6 %all-to-all-start = ((f32[8,1,2]{2,1,0:T(1,128)}), f32[8,1,2]{2,1,0:T(1,128)S(1)}, u32[]{:S(2)}, u32[]{:S(2)}) async-start(f32[8,1,2]{2,1,0:T(1,128)} %broadcast_in_dim.4), calls=%async_computation | async-start | bytes 8192 | tf_op jit(solution)/shard_map/all_to_all | solution.py:25
  64.3 4.4 %multiply_reduce_fusion = (f32[4,256]{1,0:T(4,128)S(1)}, f32[4,256,2048]{2,1,0:T(8,128)}) fusion(bf16[256,4,128]{0,2,1:T(8,128)(2,1)S(1)} %bitcast.121, f32[2048,4]{0,1:T(4,128)S(1)} %copy-done.11, bf16[2048,512]{1,0:T(8,128)(2,1)S(1)} %copy-done.4), kind=kOutput, calls=%fused_computation.34 | convolution fusion | flops 544209920 | bytes 10784768 | tf_op jit(solution)/shard_map/kli,nli->lkn/dot_general | solution.py:109
  68.7 10.2 %pmax.21 = f32[4,256]{1,0:T(4,128)S(1)} all-reduce(f32[4,256]{1,0:T(4,128)S(1)} %get-tuple-element.48), channel_id=1, replica_groups=mesh['seq_0'=4,'seq_1'=4,'seq_2'=2,'head'=8] {'seq_0'}, use_global_device_ids=true, to_apply=%region_10.0 | all-reduce | flops 1024 | bytes 8192 | tf_op jit(solution)/shard_map/pmax | solution.py:43
  78.9 8.6 %pmax.22 = f32[4,256]{1,0:T(4,128)S(1)} all-reduce(f32[4,256]{1,0:T(4,128)S(1)} %pmax.21), channel_id=1, replica_groups=mesh['seq_0'=4,'seq_1'=4,'seq_2'=2,'head'=8] {'seq_1'}, use_global_device_ids=true, to_apply=%region_11.0 | all-reduce | flops 1024 | bytes 8192 | tf_op jit(solution)/shard_map/pmax | solution.py:43
  87.5 2.5 pmax.23
  89.9 4.2 %copy.106 = f32[2048,512]{0,1:T(8,128)} copy(bf16[2048,512]{1,0:T(8,128)(2,1)} %param.9) | data formatting | bytes 6291456 | tf_op jit(solution)/shard_map/convert_element_type | solution.py:61
  94.1 2.7 %multiply_convert_fusion.1 = bf16[2048,4,128]{0,2,1:T(8,128)(2,1)S(1)} fusion(f32[2048,4,128]{0,2,1:T(8,128)} %bitcast.115, f32[2048,4]{0,1:T(4,128)S(1)} %copy-done.10), kind=kLoop, calls=%fused_computation.49 | loop fusion | flops 2097152 | bytes 6324224 | tf_op jit(solution)/shard_map/convert_element_type | solution.py:62
  96.8 5.9 %fusion.121 = bf16[256,4,128]{0,2,1:T(8,128)(2,1)} fusion(bf16[2048,4,128]{0,2,1:T(8,128)(2,1)S(1)} %multiply_convert_fusion.1, f32[4,256,2048]{2,1,0:T(8,128)} %get-tuple-element.49, f32[4,256]{1,0:T(4,128)S(1)} %pmax.23), kind=kOutput, calls=%fused_computation.148 | convolution fusion | flops 543293440 | bytes 10752000 | tf_op jit(solution)/shard_map/lnx,xlj->nlj/dot_general | solution.py:115
  102.7 0.1 fusion.164
  102.8 0.1 copy.107
  102.9 2.1 collective-permute-start
  105.0 0.1 copy.109
  105.1 1.3 collective-permute-start.1
  106.5 4.4 %fusion.2 = bf16[4,256]{1,0:T(4,128)(2,1)S(1)} fusion(f32[4,256,2048]{2,1,0:T(8,128)} %get-tuple-element.49, f32[4,256]{1,0:T(4,128)S(1)} %pmax.23), kind=kLoop, calls=%fused_computation.37 | loop fusion | flops 6290432 | bytes 8394752 | tf_op jit(solution)/shard_map/reduce_sum | solution.py:114
  110.9 4.2 %fusion.16 = f32[4,2048,256]{1,2,0:T(8,128)} fusion(bf16[256,4,128]{0,2,1:T(8,128)(2,1)S(1)} %bitcast.123, f32[2048,4]{0,1:T(4,128)S(1)} %copy-done.12, bf16[2048,512]{1,0:T(8,128)(2,1)S(1)} %copy-done.5), kind=kOutput, calls=%fused_computation.56 | convolution fusion | flops 540016640 | bytes 10780672 | tf_op jit(solution)/shard_map/zea,uea->ezu/dot_general | solution.py:130
  115.2 0.1 copy.92
  115.3 0.1 broadcast_bitcast_fusion
  115.4 0.7 fusion.166
  116.1 0.7 fusion.167
  116.7 13.5 %psum.22 = bf16[4,256]{1,0:T(4,128)(2,1)S(1)} all-reduce(bf16[4,256]{1,0:T(4,128)(2,1)S(1)} %fusion.2), channel_id=1, replica_groups=mesh['seq_0'=4,'seq_1'=4,'seq_2'=2,'head'=8] {'seq_0'}, use_global_device_ids=true, to_apply=%region_15.0 | all-reduce | flops 1024 | bytes 4096 | tf_op jit(solution)/shard_map/psum | solution.py:122
  130.2 11.7 %fusion.170 = (f32[4,2048]{1,0:T(4,128)S(1)}, f32[4,2048,256]{1,2,0:T(8,128)}) fusion(f32[4,2048,256]{1,2,0:T(8,128)} %fusion.16), kind=kOutput, calls=%fused_computation.198 | output fusion | flops 8388863 | bytes 16809984 | tf_op jit(solution)/shard_map/sub | solution.py:133
  141.9 2.5 mul.490
  144.4 5.4 %copy.108 = f32[2048,512]{1,0:T(8,128)} copy(f32[2048,512]{0,1:T(8,128)} %bitcast.116) | data formatting | bytes 8388608 | tf_op jit(solution)/shard_map/mul | solution.py:62
  149.8 4.9 %multiply_convert_fusion = bf16[2048,512]{1,0:T(8,128)(2,1)} fusion(f32[2048,512]{1,0:T(8,128)} %copy.108, bf16[2048,512]{1,0:T(8,128)(2,1)} %param.9), kind=kLoop, calls=%fused_computation.45 | loop fusion | flops 3145728 | bytes 8388608 | tf_op jit(solution)/shard_map/convert_element_type | solution.py:62
  154.7 12.4 %psum.23 = bf16[256,4]{0,1:T(4,128)(2,1)S(1)} all-reduce(bf16[256,4]{0,1:T(4,128)(2,1)S(1)} %bitcast.162), channel_id=1, replica_groups=mesh['seq_0'=4,'seq_1'=4,'seq_2'=2,'head'=8] {'seq_1','seq_2'}, use_global_device_ids=true, to_apply=%region_16.0 | all-reduce | flops 1024 | bytes 4096 | tf_op jit(solution)/shard_map/psum | solution.py:122
  167.1 0.6 fusion.168
  169.1 1.4 fusion.150
  170.5 0.5 fusion.68
  171.0 1.8 convolution_multiply_fusion.5
  172.8 4.3 %online-softmax = f32[4,256,256]{2,1,0:T(8,128)} custom-call(f32[4,256,256]{2,1,0:T(8,128)} %copy-done, f32[4,256,256]{2,1,0:T(8,128)} %convolution_multiply_fusion.5), custom_call_target="tpu_custom_call" | custom-call | tf_op online-softmax
  177.1 2.5 fusion.77
  179.7 1.4 convolution_multiply_fusion.4
  181.0 4.3 %online-softmax.1 = f32[4,256,256]{2,1,0:T(8,128)} custom-call(f32[4,256,256]{2,1,0:T(8,128)} %copy-done, f32[4,256,256]{2,1,0:T(8,128)} %convolution_multiply_fusion.4), custom_call_target="tpu_custom_call" | custom-call | tf_op online-softmax
  185.3 2.5 fusion.86
  187.9 1.4 convolution_multiply_fusion.3
  189.2 4.3 %online-softmax.2 = f32[4,256,256]{2,1,0:T(8,128)} custom-call(f32[4,256,256]{2,1,0:T(8,128)} %copy-done, f32[4,256,256]{2,1,0:T(8,128)} %convolution_multiply_fusion.3), custom_call_target="tpu_custom_call" | custom-call | tf_op online-softmax
  193.5 2.5 fusion.95
  196.1 1.4 convolution_multiply_fusion.2
  197.4 4.3 %online-softmax.3 = f32[4,256,256]{2,1,0:T(8,128)} custom-call(f32[4,256,256]{2,1,0:T(8,128)} %copy-done, f32[4,256,256]{2,1,0:T(8,128)} %convolution_multiply_fusion.2), custom_call_target="tpu_custom_call" | custom-call | tf_op online-softmax
  201.7 2.5 fusion.104
  204.3 1.4 convolution_multiply_fusion.1
  205.6 4.3 %online-softmax.4 = f32[4,256,256]{2,1,0:T(8,128)} custom-call(f32[4,256,256]{2,1,0:T(8,128)} %copy-done, f32[4,256,256]{2,1,0:T(8,128)} %convolution_multiply_fusion.1), custom_call_target="tpu_custom_call" | custom-call | tf_op online-softmax
  209.9 2.5 fusion.113
  212.5 0.0 all-reduce.2.cloned.1.call-done
  212.5 1.4 fusion.124
  213.9 6.3 %fusion.13 = f32[4,128,2048]{2,1,0:T(8,128)} fusion(bf16[256,4,128]{2,0,1:T(8,128)(2,1)S(1)} %fusion.124, f32[4,2048,256]{1,2,0:T(8,128)} %get-tuple-element.51, f32[4,2048]{1,0:T(4,128)S(1)} %get-tuple-element.50), kind=kOutput, calls=%fused_computation.54 | convolution fusion | flops 541065216 | bytes 12877824 | tf_op jit(solution)/shard_map/kbv,vkg->bkg/dot_general | solution.py:134
  220.5 5.5 %copy.94 = f32[2048,512]{1,0:T(8,128)} copy(f32[2048,512]{0,1:T(8,128)} %bitcast.119) | data formatting | bytes 8388608 | tf_op jit(solution)/shard_map/reshape | solution.py:136
  226.3 29.8 %add_convert_fusion = bf16[2048,512]{1,0:T(8,128)(2,1)} fusion(f32[2048,512]{1,0:T(8,128)} %copy.94, bf16[2048,512]{1,0:T(8,128)(2,1)S(1)} %copy-done.6, bf16[16,512]{1,0:T(8,128)(2,1)S(1)} %collective-permute-done.1, bf16[16,512]{1,0:T(8,128)(2,1)S(1)} %collective-permute-done, f32[512]{0:T(512)S(1)} %bitcast.130, f32[512]{0:T(512)S(1)} %bitcast.131, ...), kind=kLoop, calls=%fused_computation.44 | loop fusion | flops 205520896 | bytes 8488960 | tf_op jit(solution)/shard_map/convert_element_type | solution.py:147
  (109 shorter events, 0.4 us)
Async XLA Ops:
  6.5 4.7 %copy-start.12 = (f32[2048,4]{0,1:T(4,128)S(1)}, f32[2048,4]{0,1:T(4,128)}, u32[]{:S(2)}) copy-start(f32[2048,4]{0,1:T(4,128)} %param.10) | copy-start | bytes 98308
  11.3 5.0 %copy-start.4 = (bf16[2048,512]{1,0:T(8,128)(2,1)S(1)}, bf16[2048,512]{1,0:T(8,128)(2,1)}, u32[]{:S(2)}) copy-start(bf16[2048,512]{1,0:T(8,128)(2,1)} %param.8) | copy-start | bytes 6291460
  16.2 3.1 %copy-start.11 = (f32[2048,4]{0,1:T(4,128)S(1)}, f32[2048,4]{0,1:T(4,128)}, u32[]{:S(2)}) copy-start(f32[2048,4]{0,1:T(4,128)} %param.11) | copy-start | bytes 98308
  51.6 119.4 %copy-start = (f32[4,256,256]{2,1,0:T(8,128)}, f32[4,256,256]{2,1,0:T(8,128)S(1)}, u32[]{:S(2)}) copy-start(f32[4,256,256]{2,1,0:T(8,128)S(1)} %get-tuple-element.47) | copy-start | bytes 3145732
  55.7 111.4 %all-to-all-start = ((f32[8,1,2]{2,1,0:T(1,128)}), f32[8,1,2]{2,1,0:T(1,128)S(1)}, u32[]{:S(2)}, u32[]{:S(2)}) async-start(f32[8,1,2]{2,1,0:T(1,128)} %broadcast_in_dim.4), calls=%async_computation | async-start | bytes 8192 | tf_op jit(solution)/shard_map/all_to_all | solution.py:25
  64.3 148.3 %all-reduce.2.cloned.1.call-start = ((), (), s32[]{:S(2)}) async-start(), calls=%async_computation.1 | async-start | bytes 524288 | tf_op jit(solution)/shard_map/psum | solution.py:125
  68.7 25.4 %copy-start.10 = (f32[2048,4]{0,1:T(4,128)S(1)}, f32[2048,4]{0,1:T(4,128)}, u32[]{:S(2)}) copy-start(f32[2048,4]{0,1:T(4,128)} %param.12) | copy-start | bytes 98308
  102.9 123.1 %collective-permute-start = (bf16[16,512]{1,0:T(8,128)(2,1)S(1)}, bf16[16,512]{1,0:T(8,128)(2,1)S(1)}, u32[]{:S(2)}, u32[]{:S(2)}) collective-permute-start(bf16[16,512]{1,0:T(8,128)(2,1)S(1)} %copy.107), channel_id=1, source_target_pairs={{0,8},{8,16},{16,24},{24,32},{32,40},{40,48},{48,56},{56,64},{64,7... | collective-permute-start | bytes 49160 | tf_op jit(solution)/shard_map/ppermute | solution.py:53
  105.1 120.9 %collective-permute-start.1 = (bf16[16,512]{1,0:T(8,128)(2,1)S(1)}, bf16[16,512]{1,0:T(8,128)(2,1)S(1)}, u32[]{:S(2)}, u32[]{:S(2)}) collective-permute-start(bf16[16,512]{1,0:T(8,128)(2,1)S(1)} %copy.109), channel_id=1, source_target_pairs={{8,0},{16,8},{24,16},{32,24},{40,32},{48,40},{56,48},{64,56},{72,6... | collective-permute-start | bytes 49160 | tf_op jit(solution)/shard_map/ppermute | solution.py:54
  106.4 4.5 %copy-start.5 = (bf16[2048,512]{1,0:T(8,128)(2,1)S(1)}, bf16[2048,512]{1,0:T(8,128)(2,1)}, u32[]{:S(2)}) copy-start(bf16[2048,512]{1,0:T(8,128)(2,1)} %param.7) | copy-start | bytes 6291460
  106.4 4.5 %copy-start.9 = (bf16[256,512]{0,1:T(8,128)(2,1)S(1)}, bf16[256,512]{0,1:T(8,128)(2,1)}, u32[]{:S(2)}) copy-start(bf16[256,512]{0,1:T(8,128)(2,1)} %copy.112) | copy-start | bytes 786436
  110.9 4.2 %copy-start.45 = (f32[4,33]{1,0:T(4,128)S(1)}, f32[4,33]{1,0:T(4,128)}, u32[]{:S(2)}) copy-start(f32[4,33]{1,0:T(4,128)} %param.13) | copy-start | bytes 1588
  172.8 6.8 %copy-start.8 = (f32[4,256,256]{2,1,0:T(8,128)S(1)}, f32[4,256,256]{2,1,0:T(8,128)}, u32[]{:S(2)}) copy-start(f32[4,256,256]{2,1,0:T(8,128)} %convolution_multiply_fusion.5) | copy-start | bytes 3145732
  181.0 6.8 %copy-start.1 = (f32[4,256,256]{2,1,0:T(8,128)S(1)}, f32[4,256,256]{2,1,0:T(8,128)}, u32[]{:S(2)}) copy-start(f32[4,256,256]{2,1,0:T(8,128)} %convolution_multiply_fusion.4) | copy-start | bytes 3145732
  189.2 6.8 %copy-start.2 = (f32[4,256,256]{2,1,0:T(8,128)S(1)}, f32[4,256,256]{2,1,0:T(8,128)}, u32[]{:S(2)}) copy-start(f32[4,256,256]{2,1,0:T(8,128)} %convolution_multiply_fusion.3) | copy-start | bytes 3145732
  197.4 6.9 %copy-start.3 = (f32[4,256,256]{2,1,0:T(8,128)S(1)}, f32[4,256,256]{2,1,0:T(8,128)}, u32[]{:S(2)}) copy-start(f32[4,256,256]{2,1,0:T(8,128)} %convolution_multiply_fusion.2) | copy-start | bytes 3145732
  205.6 6.9 %copy-start.7 = (f32[4,256,256]{2,1,0:T(8,128)S(1)}, f32[4,256,256]{2,1,0:T(8,128)}, u32[]{:S(2)}) copy-start(f32[4,256,256]{2,1,0:T(8,128)} %convolution_multiply_fusion.1) | copy-start | bytes 3145732
  220.2 5.8 %copy-start.6 = (bf16[2048,512]{1,0:T(8,128)(2,1)S(1)}, bf16[2048,512]{1,0:T(8,128)(2,1)}, u32[]{:S(2)}) copy-start(bf16[2048,512]{1,0:T(8,128)(2,1)} %multiply_convert_fusion) | copy-start | bytes 6291460
  220.2 5.8 %copy-start.13 = (f32[512,1]{0,1:T(1,128)S(1)}, f32[512,1]{0,1:T(1,128)}, u32[]{:S(2)}) copy-start(f32[512,1]{0,1:T(1,128)} %get-tuple-element.12) | copy-start | bytes 6148
  220.2 5.8 %copy-start.14 = (f32[512,1]{0,1:T(1,128)S(1)}, f32[512,1]{0,1:T(1,128)}, u32[]{:S(2)}) copy-start(f32[512,1]{0,1:T(1,128)} %get-tuple-element.13) | copy-start | bytes 6148
  220.2 5.8 %copy-start.15 = (f32[512,1]{0,1:T(1,128)S(1)}, f32[512,1]{0,1:T(1,128)}, u32[]{:S(2)}) copy-start(f32[512,1]{0,1:T(1,128)} %get-tuple-element.14) | copy-start | bytes 6148
  220.2 5.8 %copy-start.16 = (f32[512,1]{0,1:T(1,128)S(1)}, f32[512,1]{0,1:T(1,128)}, u32[]{:S(2)}) copy-start(f32[512,1]{0,1:T(1,128)} %get-tuple-element.15) | copy-start | bytes 6148
  220.2 5.8 %copy-start.17 = (f32[512,1]{0,1:T(1,128)S(1)}, f32[512,1]{0,1:T(1,128)}, u32[]{:S(2)}) copy-start(f32[512,1]{0,1:T(1,128)} %get-tuple-element.16) | copy-start | bytes 6148
  220.2 5.8 %copy-start.18 = (f32[512,1]{0,1:T(1,128)S(1)}, f32[512,1]{0,1:T(1,128)}, u32[]{:S(2)}) copy-start(f32[512,1]{0,1:T(1,128)} %get-tuple-element.17) | copy-start | bytes 6148
  220.2 5.8 %copy-start.19 = (f32[512,1]{0,1:T(1,128)S(1)}, f32[512,1]{0,1:T(1,128)}, u32[]{:S(2)}) copy-start(f32[512,1]{0,1:T(1,128)} %get-tuple-element.18) | copy-start | bytes 6148
  220.2 5.8 %copy-start.20 = (f32[512,1]{0,1:T(1,128)S(1)}, f32[512,1]{0,1:T(1,128)}, u32[]{:S(2)}) copy-start(f32[512,1]{0,1:T(1,128)} %get-tuple-element.19) | copy-start | bytes 6148
  220.2 5.8 %copy-start.21 = (f32[512,1]{0,1:T(1,128)S(1)}, f32[512,1]{0,1:T(1,128)}, u32[]{:S(2)}) copy-start(f32[512,1]{0,1:T(1,128)} %get-tuple-element.20) | copy-start | bytes 6148
  220.3 5.8 %copy-start.22 = (f32[512,1]{0,1:T(1,128)S(1)}, f32[512,1]{0,1:T(1,128)}, u32[]{:S(2)}) copy-start(f32[512,1]{0,1:T(1,128)} %get-tuple-element.21) | copy-start | bytes 6148
  220.3 5.8 %copy-start.23 = (f32[512,1]{0,1:T(1,128)S(1)}, f32[512,1]{0,1:T(1,128)}, u32[]{:S(2)}) copy-start(f32[512,1]{0,1:T(1,128)} %get-tuple-element.22) | copy-start | bytes 6148
  220.3 5.8 %copy-start.24 = (f32[512,1]{0,1:T(1,128)S(1)}, f32[512,1]{0,1:T(1,128)}, u32[]{:S(2)}) copy-start(f32[512,1]{0,1:T(1,128)} %get-tuple-element.23) | copy-start | bytes 6148
  220.3 5.8 %copy-start.25 = (f32[512,1]{0,1:T(1,128)S(1)}, f32[512,1]{0,1:T(1,128)}, u32[]{:S(2)}) copy-start(f32[512,1]{0,1:T(1,128)} %get-tuple-element.24) | copy-start | bytes 6148
  220.3 5.8 %copy-start.26 = (f32[512,1]{0,1:T(1,128)S(1)}, f32[512,1]{0,1:T(1,128)}, u32[]{:S(2)}) copy-start(f32[512,1]{0,1:T(1,128)} %get-tuple-element.25) | copy-start | bytes 6148
  220.3 5.8 %copy-start.27 = (f32[512,1]{0,1:T(1,128)S(1)}, f32[512,1]{0,1:T(1,128)}, u32[]{:S(2)}) copy-start(f32[512,1]{0,1:T(1,128)} %get-tuple-element.26) | copy-start | bytes 6148
  220.3 5.8 %copy-start.28 = (f32[512,1]{0,1:T(1,128)S(1)}, f32[512,1]{0,1:T(1,128)}, u32[]{:S(2)}) copy-start(f32[512,1]{0,1:T(1,128)} %get-tuple-element.27) | copy-start | bytes 6148
  220.3 5.8 %copy-start.29 = (f32[512,1]{0,1:T(1,128)S(1)}, f32[512,1]{0,1:T(1,128)}, u32[]{:S(2)}) copy-start(f32[512,1]{0,1:T(1,128)} %get-tuple-element.28) | copy-start | bytes 6148
  220.3 5.8 %copy-start.30 = (f32[512,1]{0,1:T(1,128)S(1)}, f32[512,1]{0,1:T(1,128)}, u32[]{:S(2)}) copy-start(f32[512,1]{0,1:T(1,128)} %get-tuple-element.29) | copy-start | bytes 6148
  220.3 5.8 %copy-start.31 = (f32[512,1]{0,1:T(1,128)S(1)}, f32[512,1]{0,1:T(1,128)}, u32[]{:S(2)}) copy-start(f32[512,1]{0,1:T(1,128)} %get-tuple-element.30) | copy-start | bytes 6148
  220.4 5.8 %copy-start.32 = (f32[512,1]{0,1:T(1,128)S(1)}, f32[512,1]{0,1:T(1,128)}, u32[]{:S(2)}) copy-start(f32[512,1]{0,1:T(1,128)} %get-tuple-element.31) | copy-start | bytes 6148
  220.4 5.8 %copy-start.33 = (f32[512,1]{0,1:T(1,128)S(1)}, f32[512,1]{0,1:T(1,128)}, u32[]{:S(2)}) copy-start(f32[512,1]{0,1:T(1,128)} %get-tuple-element.32) | copy-start | bytes 6148
  220.4 5.8 %copy-start.34 = (f32[512,1]{0,1:T(1,128)S(1)}, f32[512,1]{0,1:T(1,128)}, u32[]{:S(2)}) copy-start(f32[512,1]{0,1:T(1,128)} %get-tuple-element.33) | copy-start | bytes 6148
  220.4 5.8 %copy-start.35 = (f32[512,1]{0,1:T(1,128)S(1)}, f32[512,1]{0,1:T(1,128)}, u32[]{:S(2)}) copy-start(f32[512,1]{0,1:T(1,128)} %get-tuple-element.34) | copy-start | bytes 6148
  220.4 5.8 %copy-start.36 = (f32[512,1]{0,1:T(1,128)S(1)}, f32[512,1]{0,1:T(1,128)}, u32[]{:S(2)}) copy-start(f32[512,1]{0,1:T(1,128)} %get-tuple-element.35) | copy-start | bytes 6148
  220.4 5.8 %copy-start.37 = (f32[512,1]{0,1:T(1,128)S(1)}, f32[512,1]{0,1:T(1,128)}, u32[]{:S(2)}) copy-start(f32[512,1]{0,1:T(1,128)} %get-tuple-element.36) | copy-start | bytes 6148
  220.4 5.8 %copy-start.38 = (f32[512,1]{0,1:T(1,128)S(1)}, f32[512,1]{0,1:T(1,128)}, u32[]{:S(2)}) copy-start(f32[512,1]{0,1:T(1,128)} %get-tuple-element.37) | copy-start | bytes 6148
  220.4 5.8 %copy-start.39 = (f32[512,1]{0,1:T(1,128)S(1)}, f32[512,1]{0,1:T(1,128)}, u32[]{:S(2)}) copy-start(f32[512,1]{0,1:T(1,128)} %get-tuple-element.38) | copy-start | bytes 6148
  220.4 5.8 %copy-start.40 = (f32[512,1]{0,1:T(1,128)S(1)}, f32[512,1]{0,1:T(1,128)}, u32[]{:S(2)}) copy-start(f32[512,1]{0,1:T(1,128)} %get-tuple-element.39) | copy-start | bytes 6148
  220.4 5.8 %copy-start.41 = (f32[512,1]{0,1:T(1,128)S(1)}, f32[512,1]{0,1:T(1,128)}, u32[]{:S(2)}) copy-start(f32[512,1]{0,1:T(1,128)} %get-tuple-element.40) | copy-start | bytes 6148
  220.5 5.8 %copy-start.42 = (f32[512,1]{0,1:T(1,128)S(1)}, f32[512,1]{0,1:T(1,128)}, u32[]{:S(2)}) copy-start(f32[512,1]{0,1:T(1,128)} %get-tuple-element.41) | copy-start | bytes 6148
  220.5 5.8 %copy-start.43 = (f32[512,1]{0,1:T(1,128)S(1)}, f32[512,1]{0,1:T(1,128)}, u32[]{:S(2)}) copy-start(f32[512,1]{0,1:T(1,128)} %get-tuple-element.42) | copy-start | bytes 6148
  220.5 5.8 %copy-start.44 = (f32[512,1]{0,1:T(1,128)S(1)}, f32[512,1]{0,1:T(1,128)}, u32[]{:S(2)}) copy-start(f32[512,1]{0,1:T(1,128)} %get-tuple-element.43) | copy-start | bytes 6148
Sparse Core Ops, SparseCore 0:
  102.8 108.5 all-reduce.1
